TPU v7x, 32 devices: a whole 2x2x4 slice. The times are simulated.
32 devices in a mesh: slab: 16 (over z, x, core), obs: 2 (over y).
Axes of the slice: x: 2, y: 2, z: 4, core: 2. Of those that a mesh axis runs over, the one named last changes fastest.
Arguments:
- background_members: float32 [64, 65536], P('slab', 'obs'), may hold values from -6 to 6
- measurement_jitter: bfloat16 [64, 2, 16384], P(None, 'obs', 'slab'), may hold values from -5 to 5
- measurement_readings: float32 [2, 16384], P('obs', 'slab'), may hold values from -8 to 8
- measurement_noise_spread: float32 [2, 16384], P('obs', 'slab'), may hold values from 0.2 to 2
- measurement_grid_location: int32 [2, 16384], P('obs', 'slab'), may hold values from 0 to 2047
- active_tallies: int32 [2, 16], P('obs', 'slab'), may hold values from 128 to 1024, as said below
- coupling_listing: int32 [2, 512, 8], P('obs', 'slab'), may hold values from 0 to 15, as said below
- taper_factors: float32 [2, 512, 8], P('obs', 'slab'), may hold values from 0.1 to 1
Outputs:
- analysis: float32 [64, 65536], P('slab', 'obs')
Inputs may be any that keep to these rules, and one draw needn't show every extreme that they name: `active_tallies`: some region of some group holds 1024 live observations; slots beyond a region's count are padding. `coupling_listing`: the 8 observation blocks listed for a state block are distinct.
All inputs are finite; a program needn't handle non-finite values.
Results may differ from a plain program's by a relative error of at most 0.0063.
Values may be sent and summed in bfloat16 or wider, within the bound.
A program may use at most 64 MiB of HBM per device.

v0:
```python
import math

import jax
import jax.numpy as jnp
from jax import lax
from jax.sharding import PartitionSpec as P

OB = 128


highest = lax.Precision.HIGHEST


def compute_increment(
    tile_work,
    measurement_jitter,
    measurement_readings,
    measurement_noise_spread,
    measurement_grid_location,
    active_tallies,
    coupling_listing,
    taper_factors,
):
    members = tile_work.shape[0]
    points = tile_work.shape[1]
    blocks = coupling_listing.shape[1]
    block_width = points // blocks
    deviation = tile_work - jnp.mean(tile_work, axis=0, keepdims=True)
    positions = measurement_grid_location[0]
    obs_count = positions.shape[0]
    prior_value = jnp.take(tile_work, positions, axis=1)
    prior_shift = prior_value - jnp.mean(prior_value, axis=0, keepdims=True)
    spread = jnp.sum(prior_shift * prior_shift, axis=0, keepdims=True) / (members - 1)
    usable = jnp.arange(obs_count, dtype=jnp.int32)[None, :] < active_tallies[0, 0]
    innovation = (
        measurement_readings + measurement_jitter[:, 0, :].astype(jnp.float32) - prior_value
    ) / (spread + measurement_noise_spread)
    gain_input = jnp.where(usable, innovation, jnp.float32(0.0)).astype(jnp.bfloat16)
    prior_low = prior_shift.astype(jnp.bfloat16)
    block_links = coupling_listing[0]
    factor = taper_factors[0] / (members - 1)
    gathered = (
        lax.all_gather(prior_low, "obs", axis=1, tiled=True),
        lax.all_gather(gain_input, "obs", axis=1, tiled=True),
    )
    all_prior = gathered[0].reshape(members, -1, OB)
    all_gain = gathered[1].reshape(members, -1, OB)
    group_size = math.gcd(blocks, 8)
    group_count = blocks // group_size

    def one_group(group_index, running):
        first_block = group_index * group_size
        local_dev = lax.dynamic_slice_in_dim(
            deviation, first_block * block_width, group_size * block_width, 1
        )
        local_dev = local_dev.reshape(members, group_size, block_width)
        chosen = lax.dynamic_slice_in_dim(block_links, first_block, group_size, 0)
        scales = lax.dynamic_slice_in_dim(factor, first_block, group_size, 0)
        picked_prior = jnp.take(all_prior, chosen, axis=1).astype(jnp.float32)
        picked_gain = jnp.take(all_gain, chosen, axis=1).astype(jnp.float32)
        covariance = jnp.einsum("mgp,mglo->glpo", local_dev, picked_prior, precision=highest)
        update = jnp.einsum("glpo,mglo,gl->mgp", covariance, picked_gain, scales, precision=highest)
        update = update.reshape(members, group_size * block_width)
        return lax.dynamic_update_slice_in_dim(running, update, first_block * block_width, 1)

    increment = lax.fori_loop(0, group_count, one_group, jnp.zeros_like(deviation))
    return increment.astype(jnp.bfloat16)


def local(
    background_members,
    measurement_jitter,
    measurement_readings,
    measurement_noise_spread,
    measurement_grid_location,
    active_tallies,
    coupling_listing,
    taper_factors,
):
    grid_segment_piece = lax.all_to_all(
        background_members, "slab", split_axis=1, concat_axis=0, tiled=True
    )
    tile_work = lax.optimization_barrier(grid_segment_piece.astype(jnp.bfloat16)).astype(
        jnp.float32
    )
    reduced_correction = compute_increment(
        tile_work,
        measurement_jitter,
        measurement_readings,
        measurement_noise_spread,
        measurement_grid_location,
        active_tallies,
        coupling_listing,
        taper_factors,
    )
    analysis = grid_segment_piece + lax.optimization_barrier(reduced_correction).astype(jnp.float32)
    return lax.all_to_all(analysis, "slab", split_axis=0, concat_axis=1, tiled=True)


def solution(mesh):
    return jax.shard_map(
        local,
        mesh=mesh,
        in_specs=(
            P("slab", "obs"),
            P(None, "obs", "slab"),
            P("obs", "slab"),
            P("obs", "slab"),
            P("obs", "slab"),
            P("obs", "slab"),
            P("obs", "slab", None),
            P("obs", "slab", None),
        ),
        out_specs=P("slab", "obs"),
        check_vma=False,
    )
```

profile of v0, /device:TPU:0, one launch (start us, length us, event | category | flops | bytes accessed | tf_op | source)
XLA Modules:
  0.0 118.8 jit_solution(4788982451282173790)
XLA Ops:
  0.0 7.4 %all-to-all-start = ((f32[4,16,2048]{2,0,1:T(4,128)}), f32[4,16,2048]{2,0,1:T(4,128)S(1)}, u32[]{:S(2)}, u32[]{:S(2)}) async-start(f32[4,16,2048]{2,0,1:T(4,128)} %bitcast.86), calls=%async_computation | async-start | bytes 1048576 | tf_op jit(solution)/shard_map/all_to_all | solution.py:80
  8.0 1.1 copy.32
  11.9 9.9 %all-to-all-done = f32[4,16,2048]{2,0,1:T(4,128)S(1)} async-done(((f32[4,16,2048]{2,0,1:T(4,128)}), f32[4,16,2048]{2,0,1:T(4,128)S(1)}, u32[]{:S(2)}, u32[]{:S(2)}) %all-to-all-start) | async-done | bytes 524320 | tf_op jit(solution)/shard_map/all_to_all | solution.py:80
  22.4 2.8 %gather_fusion.2 = f32[1024,64]{1,0:T(8,128)S(1)} fusion(f32[64,2048]{0,1:T(8,128)S(1)} %copy.33, s32[1024]{0:T(1024)S(1)} %broadcast_clamp_fusion), kind=kCustom, calls=%fused_computation.2 | custom fusion | bytes 528384 | tf_op jit(solution)/shard_map/jit(_take)/gather | solution.py:31
  27.1 8.9 %all_gather.6 = bf16[64,2048]{0,1:T(8,128)(2,1)S(1)} all-gather(bf16[64,1024]{0,1:T(8,128)(2,1)S(1)} %fusion.16), channel_id=1, replica_groups=mesh['slab'=16,'obs'=2] {'obs'}, dimensions={1}, use_global_device_ids=true | all-gather | bytes 393216 | tf_op jit(solution)/shard_map/all_gather | solution.py:44
  36.2 8.1 %all_gather.7 = bf16[64,2048]{0,1:T(8,128)(2,1)S(1)} all-gather(bf16[64,1024]{0,1:T(8,128)(2,1)S(1)} %get-tuple-element.227), channel_id=1, replica_groups=mesh['slab'=16,'obs'=2] {'obs'}, dimensions={1}, use_global_device_ids=true | all-gather | bytes 393216 | tf_op jit(solution)/shard_map/all_gather | solution.py:43
  45.4 53.5 %while.15 = (s32[]{:T(128)}, bf16[64,2048]{1,0:T(8,128)(2,1)S(1)}, s32[32,8]{1,0:T(8,128)S(1)}, bf16[64,16,128]{2,0,1:T(8,128)(2,1)S(1)}, bf16[64,16,128]{2,0,1:...) while((s32[]{:T(128)}, bf16[64,2048]{1,0:T(8,128)(2,1)S(1)}, ...), condition=%wide.region_4.6_spmd, body=%wide.region_3.5_spmd.sunk | while | flops 809502080 | bytes 13704617 | solution.py:66
  47.3 2.4 %fusion.35 = f32[8,8,128,64]{2,3,1,0:T(8,128)} fusion(f32[64,8,64,1]{0,2,3,1:T(8,128)S(1)} %bitcast.80, bf16[8,8,64,128]{3,2,1,0:T(8,128)(2,1)S(1)} %bitcast.78, pred[8,8]{1,0:T(8,128)(4,1)S(1)} %get-tuple-element.277), kind=kOutput, calls=%fused_computation.6.clone.1 | convolution fusion | flops 403177472 | bytes 3276864 | tf_op jit(solution)/shard_map/while/body/eval_jaxpr/mgp,mglo->glpo/dot_general | solution.py:61
  49.7 1.7 %gather_fusion.1 = bf16[64,64,128]{2,1,0:T(8,128)(2,1)} fusion(bf16[64,16,128]{2,0,1:T(8,128)(2,1)S(1)} %get-tuple-element.307, s32[1024]{0:T(1024)S(1)} %pad_clamp_fusion.2), kind=kCustom, calls=%fused_computation.clone.clone.1 | custom fusion | bytes 2097408 | tf_op jit(solution)/shard_map/while/body/eval_jaxpr/jit(_take)/gather | solution.py:60
  51.4 3.8 %convolution_bitcast_fusion.2 = f32[64,8,8,64]{3,0,2,1:T(8,128)S(1)} fusion(f32[8,8,128,64]{2,3,1,0:T(8,128)} %fusion.35, bf16[8,8,64,128]{3,2,1,0:T(8,128)(2,1)} %bitcast.79, pred[8,8]{1,0:T(8,128)(4,1)S(1)} %get-tuple-element.277), kind=kOutput, calls=%fused_computation.5.clone.1 | convolution fusion | flops 403177472 | bytes 4194368 | tf_op jit(solution)/shard_map/while/body/eval_jaxpr/glpo,mglo,gl->mgp/dot_general | solution.py:62
  55.3 3.1 %fusion.36 = bf16[8,1,64,64]{3,1,2,0:T(2,128)(2,1)S(1)} fusion(f32[8,8,1,1]{1,2,3,0:T(1,128)S(1)} %copy.51, f32[64,8,8,64]{3,0,2,1:T(8,128)S(1)} %convolution_bitcast_fusion.2), kind=kOutput, calls=%fused_computation.3.clone.1 | convolution fusion | flops 3145728 | bytes 1114368 | tf_op jit(solution)/shard_map/while/body/eval_jaxpr/glpo,mglo,gl->mgp/dot_general | solution.py:62
  60.7 2.4 %fusion.35 = f32[8,8,128,64]{2,3,1,0:T(8,128)} fusion(f32[64,8,64,1]{0,2,3,1:T(8,128)S(1)} %bitcast.80, bf16[8,8,64,128]{3,2,1,0:T(8,128)(2,1)S(1)} %bitcast.78, pred[8,8]{1,0:T(8,128)(4,1)S(1)} %get-tuple-element.277), kind=kOutput, calls=%fused_computation.6.clone.1 | convolution fusion | flops 403177472 | bytes 3276864 | tf_op jit(solution)/shard_map/while/body/eval_jaxpr/mgp,mglo->glpo/dot_general | solution.py:61
  63.1 1.7 %gather_fusion.1 = bf16[64,64,128]{2,1,0:T(8,128)(2,1)} fusion(bf16[64,16,128]{2,0,1:T(8,128)(2,1)S(1)} %get-tuple-element.307, s32[1024]{0:T(1024)S(1)} %pad_clamp_fusion.2), kind=kCustom, calls=%fused_computation.clone.clone.1 | custom fusion | bytes 2097408 | tf_op jit(solution)/shard_map/while/body/eval_jaxpr/jit(_take)/gather | solution.py:60
  64.7 3.8 %convolution_bitcast_fusion.2 = f32[64,8,8,64]{3,0,2,1:T(8,128)S(1)} fusion(f32[8,8,128,64]{2,3,1,0:T(8,128)} %fusion.35, bf16[8,8,64,128]{3,2,1,0:T(8,128)(2,1)} %bitcast.79, pred[8,8]{1,0:T(8,128)(4,1)S(1)} %get-tuple-element.277), kind=kOutput, calls=%fused_computation.5.clone.1 | convolution fusion | flops 403177472 | bytes 4194368 | tf_op jit(solution)/shard_map/while/body/eval_jaxpr/glpo,mglo,gl->mgp/dot_general | solution.py:62
  68.7 3.1 %fusion.36 = bf16[8,1,64,64]{3,1,2,0:T(2,128)(2,1)S(1)} fusion(f32[8,8,1,1]{1,2,3,0:T(1,128)S(1)} %copy.51, f32[64,8,8,64]{3,0,2,1:T(8,128)S(1)} %convolution_bitcast_fusion.2), kind=kOutput, calls=%fused_computation.3.clone.1 | convolution fusion | flops 3145728 | bytes 1114368 | tf_op jit(solution)/shard_map/while/body/eval_jaxpr/glpo,mglo,gl->mgp/dot_general | solution.py:62
  74.0 2.4 %fusion.35 = f32[8,8,128,64]{2,3,1,0:T(8,128)} fusion(f32[64,8,64,1]{0,2,3,1:T(8,128)S(1)} %bitcast.80, bf16[8,8,64,128]{3,2,1,0:T(8,128)(2,1)S(1)} %bitcast.78, pred[8,8]{1,0:T(8,128)(4,1)S(1)} %get-tuple-element.277), kind=kOutput, calls=%fused_computation.6.clone.1 | convolution fusion | flops 403177472 | bytes 3276864 | tf_op jit(solution)/shard_map/while/body/eval_jaxpr/mgp,mglo->glpo/dot_general | solution.py:61
  76.4 1.7 %gather_fusion.1 = bf16[64,64,128]{2,1,0:T(8,128)(2,1)} fusion(bf16[64,16,128]{2,0,1:T(8,128)(2,1)S(1)} %get-tuple-element.307, s32[1024]{0:T(1024)S(1)} %pad_clamp_fusion.2), kind=kCustom, calls=%fused_computation.clone.clone.1 | custom fusion | bytes 2097408 | tf_op jit(solution)/shard_map/while/body/eval_jaxpr/jit(_take)/gather | solution.py:60
  78.1 3.8 %convolution_bitcast_fusion.2 = f32[64,8,8,64]{3,0,2,1:T(8,128)S(1)} fusion(f32[8,8,128,64]{2,3,1,0:T(8,128)} %fusion.35, bf16[8,8,64,128]{3,2,1,0:T(8,128)(2,1)} %bitcast.79, pred[8,8]{1,0:T(8,128)(4,1)S(1)} %get-tuple-element.277), kind=kOutput, calls=%fused_computation.5.clone.1 | convolution fusion | flops 403177472 | bytes 4194368 | tf_op jit(solution)/shard_map/while/body/eval_jaxpr/glpo,mglo,gl->mgp/dot_general | solution.py:62
  82.0 3.1 %fusion.36 = bf16[8,1,64,64]{3,1,2,0:T(2,128)(2,1)S(1)} fusion(f32[8,8,1,1]{1,2,3,0:T(1,128)S(1)} %copy.51, f32[64,8,8,64]{3,0,2,1:T(8,128)S(1)} %convolution_bitcast_fusion.2), kind=kOutput, calls=%fused_computation.3.clone.1 | convolution fusion | flops 3145728 | bytes 1114368 | tf_op jit(solution)/shard_map/while/body/eval_jaxpr/glpo,mglo,gl->mgp/dot_general | solution.py:62
  87.4 2.4 %fusion.35 = f32[8,8,128,64]{2,3,1,0:T(8,128)} fusion(f32[64,8,64,1]{0,2,3,1:T(8,128)S(1)} %bitcast.80, bf16[8,8,64,128]{3,2,1,0:T(8,128)(2,1)S(1)} %bitcast.78, pred[8,8]{1,0:T(8,128)(4,1)S(1)} %get-tuple-element.277), kind=kOutput, calls=%fused_computation.6.clone.1 | convolution fusion | flops 403177472 | bytes 3276864 | tf_op jit(solution)/shard_map/while/body/eval_jaxpr/mgp,mglo->glpo/dot_general | solution.py:61
  89.8 1.7 %gather_fusion.1 = bf16[64,64,128]{2,1,0:T(8,128)(2,1)} fusion(bf16[64,16,128]{2,0,1:T(8,128)(2,1)S(1)} %get-tuple-element.307, s32[1024]{0:T(1024)S(1)} %pad_clamp_fusion.2), kind=kCustom, calls=%fused_computation.clone.clone.1 | custom fusion | bytes 2097408 | tf_op jit(solution)/shard_map/while/body/eval_jaxpr/jit(_take)/gather | solution.py:60
  91.5 3.8 %convolution_bitcast_fusion.2 = f32[64,8,8,64]{3,0,2,1:T(8,128)S(1)} fusion(f32[8,8,128,64]{2,3,1,0:T(8,128)} %fusion.35, bf16[8,8,64,128]{3,2,1,0:T(8,128)(2,1)} %bitcast.79, pred[8,8]{1,0:T(8,128)(4,1)S(1)} %get-tuple-element.277), kind=kOutput, calls=%fused_computation.5.clone.1 | convolution fusion | flops 403177472 | bytes 4194368 | tf_op jit(solution)/shard_map/while/body/eval_jaxpr/glpo,mglo,gl->mgp/dot_general | solution.py:62
  95.4 3.1 %fusion.36 = bf16[8,1,64,64]{3,1,2,0:T(2,128)(2,1)S(1)} fusion(f32[8,8,1,1]{1,2,3,0:T(1,128)S(1)} %copy.51, f32[64,8,8,64]{3,0,2,1:T(8,128)S(1)} %convolution_bitcast_fusion.2), kind=kOutput, calls=%fused_computation.3.clone.1 | convolution fusion | flops 3145728 | bytes 1114368 | tf_op jit(solution)/shard_map/while/body/eval_jaxpr/glpo,mglo,gl->mgp/dot_general | solution.py:62
  99.1 19.0 %all_to_all.38 = f32[16,4,2048]{2,1,0:T(4,128)S(1)} all-to-all(f32[16,4,2048]{2,1,0:T(4,128)S(1)} %all_to_all.32), channel_id=1, replica_groups=mesh['slab'=16,'obs'=2] {'slab'}, dimensions={0} | all-to-all | bytes 1048576 | tf_op jit(solution)/shard_map/all_to_all | solution.py:97
  (71 shorter events, 16.9 us)
Async XLA Ops:
  0.0 21.8 %all-to-all-start = ((f32[4,16,2048]{2,0,1:T(4,128)}), f32[4,16,2048]{2,0,1:T(4,128)S(1)}, u32[]{:S(2)}, u32[]{:S(2)}) async-start(f32[4,16,2048]{2,0,1:T(4,128)} %bitcast.86), calls=%async_computation | async-start | bytes 1048576 | tf_op jit(solution)/shard_map/all_to_all | solution.py:80
  22.3 3.8 %copy-start.1 = (f32[1,1024]{1,0:T(1,128)S(1)}, f32[1,1024]{1,0:T(1,128)}, u32[]{:S(2)}) copy-start(f32[1,1024]{1,0:T(1,128)} %param.15) | copy-start | bytes 12292
  22.3 3.8 %copy-start = (f32[1,1024]{1,0:T(1,128)S(1)}, f32[1,1024]{1,0:T(1,128)}, u32[]{:S(2)}) copy-start(f32[1,1024]{1,0:T(1,128)} %param.14) | copy-start | bytes 12292
where the time goes:
time: 119 us
  matrix products  37 us (31%)
  blocking collectives  35.9 us (30%)
  local copies, waits for them, and re-layouts  22.4 us (19%)
  waiting for transfers between devices  9.89 us (8%)
  starting transfers between devices  7.36 us (6%)
  other arithmetic  5.02 us (4%)
    dot_general x8, matrix products, one_group(): jnp.einsum('glpo,mglo,gl->mgp', covariance, picked_gain, scales, precisio...  27.5 us
    all_to_all x1, blocking collectives, local(): lax.all_to_all(analysis, 'slab', split_axis=0, concat_axis=1, tiled=True)  19 us
    all_to_all x1, waiting for transfers between devices, local(): lax.all_to_all(background_members, 'slab', split_axis=1, concat_axis=0, t...  9.89 us
    dot_general x4, matrix products, one_group(): jnp.einsum('mgp,mglo->glpo', local_dev, picked_prior, precision=highest)  9.58 us
    all_gather x1, blocking collectives, compute_increment(): lax.all_gather(gain_input, 'obs', axis=1, tiled=True)  8.9 us
    all_gather x1, blocking collectives, compute_increment(): lax.all_gather(prior_low, 'obs', axis=1, tiled=True)  8.05 us
    all_to_all x1, starting transfers between devices, local(): lax.all_to_all(background_members, 'slab', split_axis=1, concat_axis=0, t...  7.36 us
    gather x4, local copies, waits for them, and re-layouts, one_group(): picked_gain = jnp.take(all_gain, chosen, axis=1).astype(jnp.float32)  6.65 us
  transfers between devices with their start and end apart: 1, of which 1 were waited for; matrix products, arithmetic and copies ran while one was open for 3% of the time, Pallas kernels for 0%

commit v1 on v0

v1 whole, which is shorter than its diff:
```python
import functools

import jax
import jax.numpy as jnp
from jax import lax
from jax.experimental import pallas as pl
from jax.experimental.pallas import tpu as pltpu
from jax.sharding import PartitionSpec as P

LANES = 128
MESH = pl.DeviceIdType.MESH


def kernel(
    slabs,
    groups,
    bg,
    jitter,
    readings,
    noise,
    location,
    tally,
    coupling,
    taper,
    out,
    rows_f32,
    send1,
    recv1,
    mem_f32,
    tiles,
    dev,
    shared,
    prod,
    inc_f32,
    send2,
    recv2,
    send1_sem,
    recv1_sem,
    sendp_sem,
    recvp_sem,
    send2_sem,
    recv2_sem,
):
    own = bg.shape[0]
    span = bg.shape[1] // slabs
    cols = span // LANES
    rows = own * cols
    members = own * slabs
    half = members // 2
    chunks = location.shape[1] // LANES
    links, blocks = coupling.shape
    me = lax.axis_index("slab")
    group = lax.axis_index("obs")

    barrier = pltpu.get_barrier_semaphore()

    @pl.loop(1, slabs)
    def _(k):
        pl.semaphore_signal(
            barrier, inc=1, device_id=(lax.rem(me + k, slabs), group), device_id_type=MESH
        )

    for k in range(1, groups):
        pl.semaphore_signal(
            barrier, inc=1, device_id=(me, lax.rem(group + k, groups)), device_id_type=MESH
        )

    @pl.loop(0, slabs)
    def _(s):
        for q in range(cols):
            part = bg[:, pl.ds(pl.multiple_of(s * span + q * LANES, LANES), LANES)]
            if own == 1:
                rows_f32[pl.ds(s * rows + q, 1), :] = part
            else:
                rows_f32[pl.ds(s * rows + q, own, stride=cols), :] = part
        send1[s] = rows_f32[pl.ds(pl.multiple_of(s * rows, 16), rows), :].astype(jnp.bfloat16)

    pl.semaphore_wait(barrier, slabs - 1 + groups - 1)

    def forward(k):
        to = lax.rem(me + k, slabs)
        return pltpu.make_async_remote_copy(
            src_ref=send1.at[to],
            dst_ref=recv1.at[me],
            send_sem=send1_sem.at[to],
            recv_sem=recv1_sem.at[me],
            device_id=(to, group),
            device_id_type=MESH,
        )

    def arrived(k):
        source = lax.rem(me - k + slabs, slabs)
        return source, pltpu.make_async_remote_copy(
            src_ref=send1.at[source],
            dst_ref=recv1.at[source],
            send_sem=send1_sem.at[source],
            recv_sem=recv1_sem.at[source],
            device_id=(source, group),
            device_id_type=MESH,
        )

    @pl.loop(1, slabs)
    def _(k):
        forward(k).start()

    mem_f32[pl.ds(pl.multiple_of(me * rows, 16), rows), :] = send1[me].astype(jnp.float32)

    @pl.loop(1, slabs)
    def _(k):
        source, copy = arrived(k)
        copy.wait_recv()
        mem_f32[pl.ds(pl.multiple_of(source * rows, 16), rows), :] = recv1[source].astype(
            jnp.float32
        )

    for q in range(cols):
        tile = mem_f32[pl.ds(q, members, stride=cols), :]
        tiles[q] = tile
        dev[q] = (tile - jnp.mean(tile, axis=0, keepdims=True)).astype(jnp.bfloat16)

    live = tally[0, 0]

    @pl.loop(0, chunks)
    def _(c):
        here = pl.ds(pl.multiple_of(c * LANES, LANES), LANES)
        place = location[:, here]
        column = jnp.broadcast_to(place // LANES, (members, LANES))
        lane = jnp.broadcast_to(place % LANES, (members, LANES))
        prior = jnp.zeros((members, LANES), jnp.float32)
        for q in range(cols):
            picked = jnp.take_along_axis(tiles[q], lane, axis=1, mode="promise_in_bounds")
            prior = jnp.where(column == q, picked, prior)
        shift = prior - jnp.mean(prior, axis=0, keepdims=True)
        spread = jnp.sum(shift * shift, axis=0, keepdims=True) / (members - 1)
        innovation = (readings[:, here] + jitter[:, here].astype(jnp.float32) - prior) / (
            spread + noise[:, here]
        )
        slot = c * LANES + lax.broadcasted_iota(jnp.int32, (members, LANES), 1)
        gain = jnp.where(slot < live, innovation, 0.0).astype(jnp.bfloat16)
        product = lax.dot_general(
            gain,
            shift.astype(jnp.bfloat16),
            (((1,), (1,)), ((), ())),
            preferred_element_type=jnp.float32,
        )
        packed = jnp.concatenate([product[:half], product[half:]], axis=1)
        prod[group * chunks + c] = packed
        shared[group, c] = packed.astype(jnp.bfloat16)

    for k in range(1, groups):
        to = lax.rem(group + k, groups)
        pltpu.make_async_remote_copy(
            src_ref=shared.at[group],
            dst_ref=shared.at[group],
            send_sem=sendp_sem.at[to],
            recv_sem=recvp_sem.at[group],
            device_id=(me, to),
            device_id_type=MESH,
        ).start()
    for k in range(1, groups):
        source = lax.rem(group + k, groups)
        pltpu.make_async_remote_copy(
            src_ref=shared.at[source],
            dst_ref=shared.at[source],
            send_sem=sendp_sem.at[source],
            recv_sem=recvp_sem.at[source],
            device_id=(me, source),
            device_id_type=MESH,
        ).wait_recv()
        for c in range(chunks):
            prod[source * chunks + c] = shared[source, c].astype(jnp.float32)

    low_lane = lax.broadcasted_iota(jnp.int32, (2 * half, LANES), 1) < LANES // 2
    low_half = lax.broadcasted_iota(jnp.int32, (half, LANES), 1) < LANES // 2

    @pl.loop(0, cols)
    def _(q):
        parts = []
        for h in range(2):
            b = 2 * q + h
            total = taper[0, b] * prod[coupling[0, b]]
            for l in range(1, links):
                total = total + taper[l, b] * prod[coupling[l, b]]
            parts.append(total * (1.0 / (members - 1)))
        pair = jnp.concatenate(parts, axis=0)
        left = jnp.concatenate(
            [jnp.where(low_lane, pair, 0.0), jnp.where(low_lane, 0.0, pair)], axis=0
        ).astype(jnp.bfloat16)
        right = dev[q]
        right = jnp.concatenate([right, right], axis=0)
        update = jnp.dot(left, right, preferred_element_type=jnp.float32)
        inc_f32[pl.ds(q, half, stride=cols), :] = jnp.where(
            low_half, update[:half], update[half : 2 * half]
        )
        inc_f32[pl.ds(q + half * cols, half, stride=cols), :] = jnp.where(
            low_half, update[2 * half : 3 * half], update[3 * half :]
        )

    def backward(to):
        return pltpu.make_async_remote_copy(
            src_ref=send2.at[to],
            dst_ref=recv2.at[me],
            send_sem=send2_sem.at[to],
            recv_sem=recv2_sem.at[me],
            device_id=(to, group),
            device_id_type=MESH,
        )

    def back(source):
        return pltpu.make_async_remote_copy(
            src_ref=send2.at[source],
            dst_ref=recv2.at[source],
            send_sem=send2_sem.at[source],
            recv_sem=recv2_sem.at[source],
            device_id=(source, group),
            device_id_type=MESH,
        )

    @pl.loop(1, slabs)
    def _(k):
        to = lax.rem(me + k, slabs)
        send2[to] = inc_f32[pl.ds(pl.multiple_of(to * rows, 16), rows), :].astype(jnp.bfloat16)
        backward(to).start()

    def finish(s, low):
        rows_f32[pl.ds(pl.multiple_of(s * rows, 16), rows), :] = low.astype(jnp.float32)
        for q in range(cols):
            at = pl.ds(pl.multiple_of(s * span + q * LANES, LANES), LANES)
            if own == 1:
                part = rows_f32[pl.ds(s * rows + q, 1), :]
            else:
                part = rows_f32[pl.ds(s * rows + q, own, stride=cols), :]
            out[:, at] = bg[:, at] + part

    finish(me, inc_f32[pl.ds(pl.multiple_of(me * rows, 16), rows), :].astype(jnp.bfloat16))

    @pl.loop(1, slabs)
    def _(k):
        source = lax.rem(me - k + slabs, slabs)
        back(source).wait_recv()
        finish(source, recv2[source])

    @pl.loop(1, slabs)
    def _(k):
        forward(k).wait_send()
        backward(lax.rem(me + k, slabs)).wait_send()

    for k in range(1, groups):
        to = lax.rem(group + k, groups)
        pltpu.make_async_remote_copy(
            src_ref=shared.at[group],
            dst_ref=shared.at[group],
            send_sem=sendp_sem.at[to],
            recv_sem=recvp_sem.at[group],
            device_id=(me, to),
            device_id_type=MESH,
        ).wait_send()


def solution(mesh):
    slabs, groups = mesh.shape["slab"], mesh.shape["obs"]

    def local(
        background_members,
        measurement_jitter,
        measurement_readings,
        measurement_noise_spread,
        measurement_grid_location,
        active_tallies,
        coupling_listing,
        taper_factors,
    ):
        own, points = background_members.shape
        span = points // slabs
        cols = span // LANES
        rows = own * cols
        members = own * slabs
        slots = measurement_grid_location.shape[1]
        chunks = slots // LANES
        vmem = pl.BlockSpec(memory_space=pltpu.VMEM)
        smem = pl.BlockSpec(memory_space=pltpu.SMEM)
        f32, bf16 = jnp.float32, jnp.bfloat16
        return pl.pallas_call(
            functools.partial(kernel, slabs, groups),
            out_shape=jax.ShapeDtypeStruct((own, points), f32),
            in_specs=[vmem] * 5 + [smem] * 3,
            out_specs=vmem,
            scratch_shapes=[
                pltpu.VMEM((slabs * rows, LANES), f32),
                pltpu.VMEM((slabs, rows, LANES), bf16),
                pltpu.VMEM((slabs, rows, LANES), bf16),
                pltpu.VMEM((slabs * rows, LANES), f32),
                pltpu.VMEM((cols, members, LANES), f32),
                pltpu.VMEM((cols, members, LANES), bf16),
                pltpu.VMEM((groups, chunks, members // 2, LANES), bf16),
                pltpu.VMEM((groups * chunks, members // 2, LANES), f32),
                pltpu.VMEM((slabs * rows, LANES), f32),
                pltpu.VMEM((slabs, rows, LANES), bf16),
                pltpu.VMEM((slabs, rows, LANES), bf16),
                pltpu.SemaphoreType.DMA((slabs,)),
                pltpu.SemaphoreType.DMA((slabs,)),
                pltpu.SemaphoreType.DMA((groups,)),
                pltpu.SemaphoreType.DMA((groups,)),
                pltpu.SemaphoreType.DMA((slabs,)),
                pltpu.SemaphoreType.DMA((slabs,)),
            ],
            compiler_params=pltpu.CompilerParams(
                collective_id=0, has_side_effects=True, vmem_limit_bytes=48 * 1024 * 1024
            ),
            cost_estimate=pl.CostEstimate(
                flops=200_000_000, bytes_accessed=2_000_000, transcendentals=0
            ),
        )(
            background_members,
            measurement_jitter[:, 0, :],
            measurement_readings,
            measurement_noise_spread,
            measurement_grid_location,
            active_tallies,
            coupling_listing[0].T,
            taper_factors[0].T,
        )

    return jax.shard_map(
        local,
        mesh=mesh,
        in_specs=(
            P("slab", "obs"),
            P(None, "obs", "slab"),
            P("obs", "slab"),
            P("obs", "slab"),
            P("obs", "slab"),
            P("obs", "slab"),
            P("obs", "slab", None),
            P("obs", "slab", None),
        ),
        out_specs=P("slab", "obs"),
        check_vma=False,
    )
```

time: 119 us -> 37 us (0.31)
  matrix products: 37 us -> 0 us
  blocking collectives: 35.9 us -> 0 us
  Pallas kernels: 0 us -> 30.4 us
  local copies, waits for them, and re-layouts: 22.4 us -> 5.51 us
  waiting for transfers between devices: 9.89 us -> 0 us
  starting transfers between devices: 7.36 us -> 0 us
  other arithmetic: 5.02 us -> 0 us
    dot_general x12 -> x0, matrix products: 37 us -> none  [the longest x8 27.5 us: one_group(): jnp.einsum('glpo,mglo,gl->mgp', covariance, picked_gain, scales, precisio...]
    pallas_call x0 -> x1, Pallas kernels: none -> 30.4 us  [local(): pl.pallas_call(functools.partial(kernel, slabs, groups), out_shape=jax.Sh...]
    all_to_all x1 -> x0, blocking collectives: 19 us -> none  [local(): lax.all_to_all(analysis, 'slab', split_axis=0, concat_axis=1, tiled=True)]
    all_gather x2 -> x0, blocking collectives: 17 us -> none  [the longest x1 8.9 us: compute_increment(): lax.all_gather(gain_input, 'obs', axis=1, tiled=True)]
    gather x9 -> x0, local copies, waits for them, and re-layouts: 12.5 us -> none  [the longest x4 6.65 us: one_group(): picked_gain = jnp.take(all_gain, chosen, axis=1).astype(jnp.float32)]
    all_to_all x1 -> x0, waiting for transfers between devices: 9.89 us -> none  [local(): lax.all_to_all(background_members, 'slab', split_axis=1, concat_axis=0, t...]
    all_to_all x1 -> x0, starting transfers between devices: 7.36 us -> none  [local(): lax.all_to_all(background_members, 'slab', split_axis=1, concat_axis=0, t...]
    dynamic_slice x16 -> x0, local copies, waits for them, and re-layouts: 4.76 us -> none  [the longest x8 4.16 us: one_group(): lax.dynamic_slice_in_dim(deviation, first_block * block_width, group_size...]
  transfers between devices with their start and end apart: 1 -> 0, of which waited for: 1 -> 0; matrix products, arithmetic and copies ran while one was open for 3% -> 0% of each run, Pallas kernels for 0% -> 0%
where the time goes in v1:
time: 37 us; the launch traced here: 36.6 us
  Pallas kernels  30.4 us (82%)
  local copies, waits for them, and re-layouts  5.51 us (15%)
  between operations  0.68 us (2%)
    pallas_call x1, Pallas kernels, local(): pl.pallas_call(functools.partial(kernel, slabs, groups), out_shape=jax.Sh...  30.4 us
    unnamed x15, local copies, waits for them, and re-layouts  5.51 us

profile of v1, /device:TPU:0, one launch (start us, length us, event | category | flops | bytes accessed | tf_op | source)
XLA Modules:
  0.0 36.6 jit_solution(16044385814549123836)
XLA Ops:
  0.0 0.0 copy-start.2
  0.7 0.0 copy-done.2
  0.7 0.0 copy-start
  0.7 1.0 %copy-done = f32[4,32768]{1,0:T(4,128)S(1)} copy-done((f32[4,32768]{1,0:T(4,128)S(1)}, f32[4,32768]{1,0:T(4,128)}, u32[]{:S(2)}) %copy-start) | copy-done | bytes 524312
  1.7 0.0 copy-start.1
  1.7 0.9 %copy-done.1 = bf16[64,1,1024]{2,0,1:T(8,128)(2,1)S(1)} copy-done((bf16[64,1,1024]{2,0,1:T(8,128)(2,1)S(1)}, bf16[64,1,1024]{2,0,1:T(8,128)(2,1)}, u32[]{:S(2)}) %copy-start.1) | copy-done | bytes 131096
  2.6 0.0 copy-start.3
  2.6 0.7 %copy-done.3 = f32[1,1024]{1,0:T(1,128)S(1)} copy-done((f32[1,1024]{1,0:T(1,128)S(1)}, f32[1,1024]{1,0:T(1,128)}, u32[]{:S(2)}) %copy-start.3) | copy-done | bytes 4120
  3.3 0.0 copy-start.4
  3.3 0.7 %copy-done.4 = s32[1,1024]{1,0:T(1,128)S(1)} copy-done((s32[1,1024]{1,0:T(1,128)S(1)}, s32[1,1024]{1,0:T(1,128)}, u32[]{:S(2)}) %copy-start.4) | copy-done | bytes 4120
  4.0 0.0 copy-start.5
  4.0 0.7 %copy-done.5 = s32[1,32,8]{1,2,0:T(8,128)S(1)} copy-done((s32[1,32,8]{1,2,0:T(8,128)S(1)}, s32[1,32,8]{1,2,0:T(8,128)}, u32[]{:S(2)}) %copy-start.5) | copy-done | bytes 1048
  4.7 0.0 copy-start.6
  4.7 0.7 %copy-done.6 = f32[1,32,8]{1,2,0:T(8,128)S(1)} copy-done((f32[1,32,8]{1,2,0:T(8,128)S(1)}, f32[1,32,8]{1,2,0:T(8,128)}, u32[]{:S(2)}) %copy-start.6) | copy-done | bytes 1048
  5.4 30.4 %shard_map.82 = f32[4,32768]{1,0:T(4,128)S(1)} custom-call(f32[4,32768]{1,0:T(4,128)S(1)} %copy-done, bf16[64,1024]{1,0:T(8,128)(2,1)S(1)} %bitcast.7, f32[1,1024]{1,0:T(1,128)S(1)} %copy-done.2, f32[1,1024]{1,0:T(1,128)S(1)} %copy-done.3, s32[1,1024]{1,0:T(1,128)S(1)} %copy-done.4, s32[1,1]{1,0:T(1,128)S(6)} %copy.10.tally, s32[8,32]{1,0:T(8,128)S(1)} %bitcast.8, ...), custom_call_target="tpu_custom_call" | custom-call | flops 200000000 | bytes 2000000 | tf_op jit(solution)/shard_map/pallas_call | solution.py:283
  35.8 0.8 %copy.11 = f32[4,32768]{1,0:T(4,128)} copy(f32[4,32768]{1,0:T(4,128)S(1)} %shard_map.82) | data formatting | bytes 1048576
Async XLA Ops:
  0.0 0.7 %copy-start.2 = (f32[1,1024]{1,0:T(1,128)S(1)}, f32[1,1024]{1,0:T(1,128)}, u32[]{:S(2)}) copy-start(f32[1,1024]{1,0:T(1,128)} %readings.1) | copy-start | bytes 12292
  0.7 1.0 %copy-start = (f32[4,32768]{1,0:T(4,128)S(1)}, f32[4,32768]{1,0:T(4,128)}, u32[]{:S(2)}) copy-start(f32[4,32768]{1,0:T(4,128)} %bg.1) | copy-start | bytes 1572868
  1.7 0.9 %copy-start.1 = (bf16[64,1,1024]{2,0,1:T(8,128)(2,1)S(1)}, bf16[64,1,1024]{2,0,1:T(8,128)(2,1)}, u32[]{:S(2)}) copy-start(bf16[64,1,1024]{2,0,1:T(8,128)(2,1)} %param.9) | copy-start | bytes 393220
  2.6 0.7 %copy-start.3 = (f32[1,1024]{1,0:T(1,128)S(1)}, f32[1,1024]{1,0:T(1,128)}, u32[]{:S(2)}) copy-start(f32[1,1024]{1,0:T(1,128)} %noise.1) | copy-start | bytes 12292
  3.3 0.7 %copy-start.4 = (s32[1,1024]{1,0:T(1,128)S(1)}, s32[1,1024]{1,0:T(1,128)}, u32[]{:S(2)}) copy-start(s32[1,1024]{1,0:T(1,128)} %location.1) | copy-start | bytes 12292
  4.0 0.7 %copy-start.5 = (s32[1,32,8]{1,2,0:T(8,128)S(1)}, s32[1,32,8]{1,2,0:T(8,128)}, u32[]{:S(2)}) copy-start(s32[1,32,8]{1,2,0:T(8,128)} %param.14) | copy-start | bytes 3076
  4.7 0.7 %copy-start.6 = (f32[1,32,8]{1,2,0:T(8,128)S(1)}, f32[1,32,8]{1,2,0:T(8,128)}, u32[]{:S(2)}) copy-start(f32[1,32,8]{1,2,0:T(8,128)} %param.15) | copy-start | bytes 3076

commit v2 on v1

v2 whole, which is shorter than its diff:
```python
import functools

import jax
import jax.numpy as jnp
from jax import lax
from jax.experimental import pallas as pl
from jax.experimental.pallas import tpu as pltpu
from jax.sharding import PartitionSpec as P

LANES = 128
MESH = pl.DeviceIdType.MESH


def kernel(
    slabs,
    groups,
    parts,
    bg_hbm,
    jitter_hbm,
    readings_hbm,
    noise_hbm,
    location_hbm,
    tally,
    coupling_hbm,
    taper_hbm,
    out_hbm,
    out,
    bg,
    jitter,
    readings,
    noise,
    location,
    coupling,
    taper,
    rows_f32,
    send1,
    recv1,
    mem_f32,
    tiles,
    prior_all,
    dev,
    shared,
    prod,
    inc_f32,
    send2,
    recv2,
    bg_sem,
    load_sem,
    send1_sem,
    recv1_sem,
    sendp_sem,
    recvp_sem,
    send2_sem,
    recv2_sem,
    out_sem,
):
    own = bg.shape[0]
    span = bg.shape[1] // slabs
    cols = span // LANES
    rows = own * cols
    members = own * slabs
    half = members // 2
    chunks = location.shape[1] // LANES
    links, blocks = coupling.shape
    bundles = members // 8
    per = slabs // bundles
    part_cols = cols // parts
    part_rows = own * part_cols
    me = lax.axis_index("slab")
    group = lax.axis_index("obs")
    home = me // per

    barrier = pltpu.get_barrier_semaphore()

    def bg_load(v):
        at = pl.ds(pl.multiple_of(v * per * span, LANES), per * span)
        return pltpu.make_async_copy(bg_hbm.at[:, at], bg.at[:, at], bg_sem.at[v])

    @pl.loop(0, bundles)
    def _(v):
        bg_load(v).start()

    loads = [
        pltpu.make_async_copy(source, target, load_sem.at[i])
        for i, (source, target) in enumerate(
            (
                (location_hbm, location),
                (jitter_hbm, jitter),
                (readings_hbm, readings),
                (noise_hbm, noise),
                (coupling_hbm, coupling),
                (taper_hbm, taper),
            )
        )
    ]
    for load in loads:
        load.start()

    @pl.loop(1, slabs)
    def _(k):
        pl.semaphore_signal(
            barrier, inc=1, device_id=(lax.rem(me + k, slabs), group), device_id_type=MESH
        )

    for k in range(1, groups):
        pl.semaphore_signal(
            barrier, inc=1, device_id=(me, lax.rem(group + k, groups)), device_id_type=MESH
        )

    @pl.loop(0, bundles)
    def _(v):
        bg_load(v).wait()
        for j in range(per):
            s = v * per + j
            for q in range(cols):
                part = bg[:, pl.ds(pl.multiple_of(s * span + q * LANES, LANES), LANES)]
                if own == 1:
                    rows_f32[pl.ds(s * rows + q, 1), :] = part
                else:
                    rows_f32[pl.ds(s * rows + q, own, stride=cols), :] = part
            send1[s] = rows_f32[pl.ds(pl.multiple_of(s * rows, 16), rows), :].astype(jnp.bfloat16)

    pl.semaphore_wait(barrier, slabs - 1 + groups - 1)

    def forward(to):
        return pltpu.make_async_remote_copy(
            src_ref=send1.at[to],
            dst_ref=recv1.at[me],
            send_sem=send1_sem.at[to],
            recv_sem=recv1_sem.at[me],
            device_id=(to, group),
            device_id_type=MESH,
        )

    def arriving(source):
        return pltpu.make_async_remote_copy(
            src_ref=send1.at[source],
            dst_ref=recv1.at[source],
            send_sem=send1_sem.at[source],
            recv_sem=recv1_sem.at[source],
            device_id=(source, group),
            device_id_type=MESH,
        )

    @pl.loop(1, slabs)
    def _(k):
        forward(lax.rem(me + slabs - k, slabs)).start()

    recv1[me] = send1[me]

    loads[0].wait()
    place = location[...]
    column = [
        jnp.broadcast_to(place[:, c * LANES : (c + 1) * LANES] >> 7, (8, LANES))
        for c in range(chunks)
    ]
    lane = [
        jnp.broadcast_to(place[:, c * LANES : (c + 1) * LANES] & (LANES - 1), (8, LANES))
        for c in range(chunks)
    ]

    @pl.loop(0, bundles)
    def _(k):
        v = lax.rem(home + k, bundles)
        for j in range(per):
            source = v * per + j

            @pl.when(source != me)
            def _():
                arriving(source).wait_recv()

            mem_f32[pl.ds(pl.multiple_of(source * rows, 16), rows), :] = recv1[source].astype(
                jnp.float32
            )
        eight = pl.ds(pl.multiple_of(v * 8, 8), 8)
        values = [jnp.zeros((8, LANES), jnp.float32)] * chunks
        for q in range(cols):
            tile = mem_f32[pl.ds(v * 8 * cols + q, 8, stride=cols), :]
            tiles[q, eight, :] = tile
            for c in range(chunks):
                picked = jnp.take_along_axis(tile, lane[c], axis=1, mode="promise_in_bounds")
                values[c] = jnp.where(column[c] == q, picked, values[c])
        for c in range(chunks):
            prior_all[c, eight, :] = values[c]

    def share(c, to, owner):
        return pltpu.make_async_remote_copy(
            src_ref=shared.at[owner, c],
            dst_ref=shared.at[owner, c],
            send_sem=sendp_sem.at[to, c],
            recv_sem=recvp_sem.at[owner, c],
            device_id=(me, to),
            device_id_type=MESH,
        )

    for load in loads[1:]:
        load.wait()
    live = tally[0, 0]
    lanes = lax.broadcasted_iota(jnp.int32, (members, LANES), 1)
    for c in range(chunks):
        here = slice(c * LANES, (c + 1) * LANES)
        prior = prior_all[c]
        shift = prior - jnp.mean(prior, axis=0, keepdims=True)
        spread = jnp.sum(shift * shift, axis=0, keepdims=True) * (1.0 / (members - 1))
        innovation = (readings[:, here] + jitter[:, here].astype(jnp.float32) - prior) * (
            1.0 / (spread + noise[:, here])
        )
        gain = jnp.where(lanes + c * LANES < live, innovation, 0.0).astype(jnp.bfloat16)
        product = lax.dot_general(
            gain,
            shift.astype(jnp.bfloat16),
            (((1,), (1,)), ((), ())),
            preferred_element_type=jnp.float32,
        )
        packed = jnp.concatenate([product[:half], product[half:]], axis=1)
        prod[group * chunks + c] = packed
        shared[group, c] = packed.astype(jnp.bfloat16)
        for k in range(1, groups):
            share(c, lax.rem(group + k, groups), group).start()

    for q in range(cols):
        tile = tiles[q]
        dev[q] = (tile - jnp.mean(tile, axis=0, keepdims=True)).astype(jnp.bfloat16)

    for k in range(1, groups):
        source = lax.rem(group + k, groups)
        for c in range(chunks):
            share(c, source, source).wait_recv()
            prod[source * chunks + c] = shared[source, c].astype(jnp.float32)

    low_lane = lax.broadcasted_iota(jnp.int32, (2 * half, LANES), 1) < LANES // 2
    low_half = lax.broadcasted_iota(jnp.int32, (half, LANES), 1) < LANES // 2

    def backward(h, to):
        return pltpu.make_async_remote_copy(
            src_ref=send2.at[h, to],
            dst_ref=recv2.at[h, me],
            send_sem=send2_sem.at[h, to],
            recv_sem=recv2_sem.at[h, me],
            device_id=(to, group),
            device_id_type=MESH,
        )

    def back(h, source):
        return pltpu.make_async_remote_copy(
            src_ref=send2.at[h, source],
            dst_ref=recv2.at[h, source],
            send_sem=send2_sem.at[h, source],
            recv_sem=recv2_sem.at[h, source],
            device_id=(source, group),
            device_id_type=MESH,
        )

    for h in range(parts):
        for i in range(part_cols):
            q = h * part_cols + i
            pair = []
            for b in (2 * q, 2 * q + 1):
                total = taper[0, b] * prod[coupling[0, b]]
                for l in range(1, links):
                    total = total + taper[l, b] * prod[coupling[l, b]]
                pair.append(total * (1.0 / (members - 1)))
            pair = jnp.concatenate(pair, axis=0)
            left = jnp.concatenate(
                [jnp.where(low_lane, pair, 0.0), jnp.where(low_lane, 0.0, pair)], axis=0
            ).astype(jnp.bfloat16)
            right = dev[q]
            right = jnp.concatenate([right, right], axis=0)
            update = jnp.dot(left, right, preferred_element_type=jnp.float32)
            inc_f32[h, pl.ds(i, half, stride=part_cols), :] = jnp.where(
                low_half, update[:half], update[half : 2 * half]
            )
            inc_f32[h, pl.ds(i + half * part_cols, half, stride=part_cols), :] = jnp.where(
                low_half, update[2 * half : 3 * half], update[3 * half :]
            )

        @pl.loop(1, slabs)
        def _(k):
            to = lax.rem(me + slabs - k, slabs)
            send2[h, to] = inc_f32[
                h, pl.ds(pl.multiple_of(to * part_rows, 16), part_rows), :
            ].astype(jnp.bfloat16)
            backward(h, to).start()

    def finish(h, s, low):
        base = s * rows + h * part_rows
        rows_f32[pl.ds(pl.multiple_of(base, 16), part_rows), :] = low.astype(jnp.float32)
        for i in range(part_cols):
            q = h * part_cols + i
            at = pl.ds(pl.multiple_of(s * span + q * LANES, LANES), LANES)
            if own == 1:
                part = rows_f32[pl.ds(base + i, 1), :]
            else:
                part = rows_f32[pl.ds(base + i, own, stride=part_cols), :]
            out[:, at] = bg[:, at] + part

    def out_copy(s):
        at = pl.ds(pl.multiple_of(s * span, LANES), span)
        return pltpu.make_async_copy(out.at[:, at], out_hbm.at[:, at], out_sem.at[s])

    for h in range(parts):
        finish(
            h,
            me,
            inc_f32[h, pl.ds(pl.multiple_of(me * part_rows, 16), part_rows), :].astype(
                jnp.bfloat16
            ),
        )
        if h == parts - 1:
            out_copy(me).start()

        @pl.loop(1, slabs)
        def _(k):
            source = lax.rem(me + k, slabs)
            back(h, source).wait_recv()
            finish(h, source, recv2[h, source])
            if h == parts - 1:
                out_copy(source).start()

    @pl.loop(1, slabs)
    def _(k):
        to = lax.rem(me + k, slabs)
        forward(to).wait_send()
        for h in range(parts):
            backward(h, to).wait_send()
        out_copy(to).wait()

    out_copy(me).wait()

    for k in range(1, groups):
        to = lax.rem(group + k, groups)
        for c in range(chunks):
            share(c, to, group).wait_send()


def solution(mesh):
    slabs, groups = mesh.shape["slab"], mesh.shape["obs"]

    def local(
        background_members,
        measurement_jitter,
        measurement_readings,
        measurement_noise_spread,
        measurement_grid_location,
        active_tallies,
        coupling_listing,
        taper_factors,
    ):
        own, points = background_members.shape
        span = points // slabs
        cols = span // LANES
        rows = own * cols
        members = own * slabs
        slots = measurement_grid_location.shape[1]
        chunks = slots // LANES
        blocks, links = coupling_listing.shape[1:]
        parts = 2 if rows % 32 == 0 else 1
        smem = pl.BlockSpec(memory_space=pltpu.SMEM)
        hbm = pl.BlockSpec(memory_space=pl.ANY)
        f32, bf16, i32 = jnp.float32, jnp.bfloat16, jnp.int32
        return pl.pallas_call(
            functools.partial(kernel, slabs, groups, parts),
            out_shape=jax.ShapeDtypeStruct((own, points), f32),
            in_specs=[hbm] * 5 + [smem] + [hbm] * 2,
            out_specs=hbm,
            scratch_shapes=[
                pltpu.VMEM((own, points), f32),
                pltpu.VMEM((own, points), f32),
                pltpu.VMEM((members, slots), bf16),
                pltpu.VMEM((1, slots), f32),
                pltpu.VMEM((1, slots), f32),
                pltpu.VMEM((1, slots), i32),
                pltpu.SMEM((links, blocks), i32),
                pltpu.SMEM((links, blocks), f32),
                pltpu.VMEM((slabs * rows, LANES), f32),
                pltpu.VMEM((slabs, rows, LANES), bf16),
                pltpu.VMEM((slabs, rows, LANES), bf16),
                pltpu.VMEM((slabs * rows, LANES), f32),
                pltpu.VMEM((cols, members, LANES), f32),
                pltpu.VMEM((chunks, members, LANES), f32),
                pltpu.VMEM((cols, members, LANES), bf16),
                pltpu.VMEM((groups, chunks, members // 2, LANES), bf16),
                pltpu.VMEM((groups * chunks, members // 2, LANES), f32),
                pltpu.VMEM((parts, slabs * rows // parts, LANES), f32),
                pltpu.VMEM((parts, slabs, rows // parts, LANES), bf16),
                pltpu.VMEM((parts, slabs, rows // parts, LANES), bf16),
                pltpu.SemaphoreType.DMA((members // 8,)),
                pltpu.SemaphoreType.DMA((6,)),
                pltpu.SemaphoreType.DMA((slabs,)),
                pltpu.SemaphoreType.DMA((slabs,)),
                pltpu.SemaphoreType.DMA((groups, chunks)),
                pltpu.SemaphoreType.DMA((groups, chunks)),
                pltpu.SemaphoreType.DMA((parts, slabs)),
                pltpu.SemaphoreType.DMA((parts, slabs)),
                pltpu.SemaphoreType.DMA((slabs,)),
            ],
            compiler_params=pltpu.CompilerParams(
                collective_id=0, has_side_effects=True, vmem_limit_bytes=60 * 1024 * 1024
            ),
            cost_estimate=pl.CostEstimate(
                flops=200_000_000, bytes_accessed=2_000_000, transcendentals=0
            ),
        )(
            background_members,
            measurement_jitter[:, 0, :],
            measurement_readings,
            measurement_noise_spread,
            measurement_grid_location,
            active_tallies,
            coupling_listing[0].T,
            taper_factors[0].T,
        )

    return jax.shard_map(
        local,
        mesh=mesh,
        in_specs=(
            P("slab", "obs"),
            P(None, "obs", "slab"),
            P("obs", "slab"),
            P("obs", "slab"),
            P("obs", "slab"),
            P("obs", "slab"),
            P("obs", "slab", None),
            P("obs", "slab", None),
        ),
        out_specs=P("slab", "obs"),
        check_vma=False,
    )
```

time: 37 us -> 32 us (0.86)
  local copies, waits for them, and re-layouts: 5.51 us -> 1.87 us
  Pallas kernels: 30.4 us -> 29.3 us
    unnamed x15 -> x1, local copies, waits for them, and re-layouts: 5.51 us -> 1.87 us
    pallas_call x1, Pallas kernels: 30.4 us -> 29.3 us  [local(): pl.pallas_call(functools.partial(kernel, slabs, groups, parts), out_shape...]
where the time goes in v2:
time: 32 us; the launch traced here: 31.8 us
  Pallas kernels  29.3 us (92%)
  local copies, waits for them, and re-layouts  1.87 us (6%)
  between operations  0.66 us (2%)
    pallas_call x1, Pallas kernels, local(): pl.pallas_call(functools.partial(kernel, slabs, groups, parts), out_shape...  29.3 us
    unnamed x1, local copies, waits for them, and re-layouts  1.87 us

profile of v2, /device:TPU:0, one launch (start us, length us, event | category | flops | bytes accessed | tf_op | source)
XLA Modules:
  0.0 31.8 jit_solution(11240288539589466368)
XLA Ops:
  0.7 29.3 %shard_map.82 = f32[4,32768]{1,0:T(4,128)} custom-call(f32[4,32768]{1,0:T(4,128)} %bg_hbm.1, bf16[64,1024]{1,0:T(8,128)(2,1)} %bitcast.7, f32[1,1024]{1,0:T(1,128)} %readings_hbm.1, f32[1,1024]{1,0:T(1,128)} %noise_hbm.1, s32[1,1024]{1,0:T(1,128)} %location_hbm.1, s32[1,1]{1,0:T(1,128)S(6)} %copy.10.tally, s32[8,32]{1,0:T(8,128)} %bitcast.8, f32[8,32]{1,0:T(8,128)} %bitcast.9), custom_call_target="tpu_custom_call" | custom-call | flops 200000000 | bytes 2000000 | tf_op jit(solution)/shard_map/pallas_call | solution.py:361
  29.9 1.9 %copy.11 = f32[4,32768]{1,0:T(4,128)} copy(f32[4,32768]{1,0:T(4,128)} %shard_map.82) | data formatting | bytes 1048576

commit v3 on v2

--- a/solution.py
+++ b/solution.py
@@ -23,7 +23,6 @@
     tally,
     coupling_hbm,
     taper_hbm,
-    out_hbm,
     out,
     bg,
     jitter,
@@ -52,7 +51,6 @@
     recvp_sem,
     send2_sem,
     recv2_sem,
-    out_sem,
 ):
     own = bg.shape[0]
     span = bg.shape[1] // slabs
@@ -72,13 +70,24 @@
 
     barrier = pltpu.get_barrier_semaphore()
 
+    @pl.loop(1, slabs)
+    def _(k):
+        pl.semaphore_signal(
+            barrier, inc=1, device_id=(lax.rem(me + k, slabs), group), device_id_type=MESH
+        )
+
+    for k in range(1, groups):
+        pl.semaphore_signal(
+            barrier, inc=1, device_id=(me, lax.rem(group + k, groups)), device_id_type=MESH
+        )
+
     def bg_load(v):
         at = pl.ds(pl.multiple_of(v * per * span, LANES), per * span)
         return pltpu.make_async_copy(bg_hbm.at[:, at], bg.at[:, at], bg_sem.at[v])
 
     @pl.loop(0, bundles)
-    def _(v):
-        bg_load(v).start()
+    def _(k):
+        bg_load(lax.rem(home + 2 * bundles - 1 - k, bundles)).start()
 
     loads = [
         pltpu.make_async_copy(source, target, load_sem.at[i])
@@ -96,19 +105,28 @@
     for load in loads:
         load.start()
 
-    @pl.loop(1, slabs)
-    def _(k):
-        pl.semaphore_signal(
-            barrier, inc=1, device_id=(lax.rem(me + k, slabs), group), device_id_type=MESH
-        )
-
-    for k in range(1, groups):
-        pl.semaphore_signal(
-            barrier, inc=1, device_id=(me, lax.rem(group + k, groups)), device_id_type=MESH
-        )
-
-    @pl.loop(0, bundles)
-    def _(v):
+    def forward(to):
+        return pltpu.make_async_remote_copy(
+            src_ref=send1.at[to],
+            dst_ref=recv1.at[me],
+            send_sem=send1_sem.at[to],
+            recv_sem=recv1_sem.at[me],
+            device_id=(to, group),
+            device_id_type=MESH,
+        )
+
+    def arriving(source):
+        return pltpu.make_async_remote_copy(
+            src_ref=send1.at[source],
+            dst_ref=recv1.at[source],
+            send_sem=send1_sem.at[source],
+            recv_sem=recv1_sem.at[source],
+            device_id=(source, group),
+            device_id_type=MESH,
+        )
+
+    def pack(k):
+        v = lax.rem(home + 2 * bundles - 1 - k, bundles)
         bg_load(v).wait()
         for j in range(per):
             s = v * per + j
@@ -120,31 +138,31 @@
                     rows_f32[pl.ds(s * rows + q, own, stride=cols), :] = part
             send1[s] = rows_f32[pl.ds(pl.multiple_of(s * rows, 16), rows), :].astype(jnp.bfloat16)
 
+    def send(k):
+        v = lax.rem(home + 2 * bundles - 1 - k, bundles)
+        for j in range(per):
+            to = v * per + j
+
+            @pl.when(to != me)
+            def _():
+                forward(to).start()
+
+    early = 2
+
+    @pl.loop(0, early)
+    def _(k):
+        pack(k)
+
     pl.semaphore_wait(barrier, slabs - 1 + groups - 1)
 
-    def forward(to):
-        return pltpu.make_async_remote_copy(
-            src_ref=send1.at[to],
-            dst_ref=recv1.at[me],
-            send_sem=send1_sem.at[to],
-            recv_sem=recv1_sem.at[me],
-            device_id=(to, group),
-            device_id_type=MESH,
-        )
-
-    def arriving(source):
-        return pltpu.make_async_remote_copy(
-            src_ref=send1.at[source],
-            dst_ref=recv1.at[source],
-            send_sem=send1_sem.at[source],
-            recv_sem=recv1_sem.at[source],
-            device_id=(source, group),
-            device_id_type=MESH,
-        )
-
-    @pl.loop(1, slabs)
-    def _(k):
-        forward(lax.rem(me + slabs - k, slabs)).start()
+    @pl.loop(0, early)
+    def _(k):
+        send(k)
+
+    @pl.loop(early, bundles)
+    def _(k):
+        pack(k)
+        send(k)
 
     recv1[me] = send1[me]
 
@@ -161,7 +179,7 @@
 
     @pl.loop(0, bundles)
     def _(k):
-        v = lax.rem(home + k, bundles)
+        v = lax.rem(home + 1 + k, bundles)
         for j in range(per):
             source = v * per + j
 
@@ -294,10 +312,6 @@
                 part = rows_f32[pl.ds(base + i, own, stride=part_cols), :]
             out[:, at] = bg[:, at] + part
 
-    def out_copy(s):
-        at = pl.ds(pl.multiple_of(s * span, LANES), span)
-        return pltpu.make_async_copy(out.at[:, at], out_hbm.at[:, at], out_sem.at[s])
-
     for h in range(parts):
         finish(
             h,
@@ -306,16 +320,12 @@
                 jnp.bfloat16
             ),
         )
-        if h == parts - 1:
-            out_copy(me).start()
 
         @pl.loop(1, slabs)
         def _(k):
             source = lax.rem(me + k, slabs)
             back(h, source).wait_recv()
             finish(h, source, recv2[h, source])
-            if h == parts - 1:
-                out_copy(source).start()
 
     @pl.loop(1, slabs)
     def _(k):
@@ -323,9 +333,6 @@
         forward(to).wait_send()
         for h in range(parts):
             backward(h, to).wait_send()
-        out_copy(to).wait()
-
-    out_copy(me).wait()
 
     for k in range(1, groups):
         to = lax.rem(group + k, groups)
@@ -360,11 +367,10 @@
         f32, bf16, i32 = jnp.float32, jnp.bfloat16, jnp.int32
         return pl.pallas_call(
             functools.partial(kernel, slabs, groups, parts),
-            out_shape=jax.ShapeDtypeStruct((own, points), f32),
+            out_shape=pltpu.VMEM((own, points), f32),
             in_specs=[hbm] * 5 + [smem] + [hbm] * 2,
-            out_specs=hbm,
+            out_specs=pl.BlockSpec(memory_space=pltpu.VMEM),
             scratch_shapes=[
-                pltpu.VMEM((own, points), f32),
                 pltpu.VMEM((own, points), f32),
                 pltpu.VMEM((members, slots), bf16),
                 pltpu.VMEM((1, slots), f32),
@@ -392,7 +398,6 @@
                 pltpu.SemaphoreType.DMA((groups, chunks)),
                 pltpu.SemaphoreType.DMA((parts, slabs)),
                 pltpu.SemaphoreType.DMA((parts, slabs)),
-                pltpu.SemaphoreType.DMA((slabs,)),
             ],
             compiler_params=pltpu.CompilerParams(
                 collective_id=0, has_side_effects=True, vmem_limit_bytes=60 * 1024 * 1024

time: 32 us -> 31.4 us (0.981)
  local copies, waits for them, and re-layouts: 1.87 us -> 0.8 us
  Pallas kernels: 29.3 us -> 29.8 us
    unnamed x1, local copies, waits for them, and re-layouts: 1.87 us -> 0.8 us
    pallas_call x1, Pallas kernels: 29.3 us -> 29.8 us  [local(): pl.pallas_call(functools.partial(kernel, slabs, groups, parts), out_shape...]
where the time goes in v3:
time: 31.4 us; the launch traced here: 31.2 us
  Pallas kernels  29.8 us (95%)
  local copies, waits for them, and re-layouts  0.8 us (3%)
  between operations  0.66 us (2%)
    pallas_call x1, Pallas kernels, local(): pl.pallas_call(functools.partial(kernel, slabs, groups, parts), out_shape...  29.8 us
    unnamed x1, local copies, waits for them, and re-layouts  0.8 us

profile of v3, /device:TPU:0, one launch (start us, length us, event | category | flops | bytes accessed | tf_op | source)
XLA Modules:
  0.0 31.2 jit_solution(16037036287985394962)
XLA Ops:
  0.7 29.8 %shard_map.82 = f32[4,32768]{1,0:T(4,128)S(1)} custom-call(f32[4,32768]{1,0:T(4,128)} %bg_hbm.1, bf16[64,1024]{1,0:T(8,128)(2,1)} %bitcast.7, f32[1,1024]{1,0:T(1,128)} %readings_hbm.1, f32[1,1024]{1,0:T(1,128)} %noise_hbm.1, s32[1,1024]{1,0:T(1,128)} %location_hbm.1, s32[1,1]{1,0:T(1,128)S(6)} %copy.11.tally, s32[8,32]{1,0:T(8,128)} %bitcast.8, f32[8,32]{1,0:T(8,128)} %bitcast.9), custom_call_target="tpu_custom_call" | custom-call | flops 200000000 | bytes 2000000 | tf_op jit(solution)/shard_map/pallas_call | solution.py:368
  30.4 0.8 %copy.10 = f32[4,32768]{1,0:T(4,128)} copy(f32[4,32768]{1,0:T(4,128)S(1)} %shard_map.82) | data formatting | bytes 1048576

commit v4 on v3

--- a/solution.py
+++ b/solution.py
@@ -67,6 +67,17 @@
     me = lax.axis_index("slab")
     group = lax.axis_index("obs")
     home = me // per
+    depth = bundles // 2
+
+    def ahead(k):
+        j = lax.rem(k + 2, bundles)
+        z = lax.rem(home // 2 + depth - j // 2, depth)
+        return z * 2 + lax.rem(home + j, 2)
+
+    def behind(k):
+        j = lax.rem(k + 2, bundles)
+        z = lax.rem(home // 2 + j // 2, depth)
+        return z * 2 + lax.rem(home + j, 2)
 
     barrier = pltpu.get_barrier_semaphore()
 
@@ -87,7 +98,7 @@
 
     @pl.loop(0, bundles)
     def _(k):
-        bg_load(lax.rem(home + 2 * bundles - 1 - k, bundles)).start()
+        bg_load(ahead(k)).start()
 
     loads = [
         pltpu.make_async_copy(source, target, load_sem.at[i])
@@ -126,7 +137,7 @@
         )
 
     def pack(k):
-        v = lax.rem(home + 2 * bundles - 1 - k, bundles)
+        v = ahead(k)
         bg_load(v).wait()
         for j in range(per):
             s = v * per + j
@@ -139,7 +150,7 @@
             send1[s] = rows_f32[pl.ds(pl.multiple_of(s * rows, 16), rows), :].astype(jnp.bfloat16)
 
     def send(k):
-        v = lax.rem(home + 2 * bundles - 1 - k, bundles)
+        v = ahead(k)
         for j in range(per):
             to = v * per + j
 
@@ -147,21 +158,14 @@
             def _():
                 forward(to).start()
 
-    early = 2
-
-    @pl.loop(0, early)
+    @pl.loop(0, bundles)
     def _(k):
         pack(k)
 
     pl.semaphore_wait(barrier, slabs - 1 + groups - 1)
 
-    @pl.loop(0, early)
-    def _(k):
-        send(k)
-
-    @pl.loop(early, bundles)
-    def _(k):
-        pack(k)
+    @pl.loop(0, bundles)
+    def _(k):
         send(k)
 
     recv1[me] = send1[me]
@@ -179,7 +183,7 @@
 
     @pl.loop(0, bundles)
     def _(k):
-        v = lax.rem(home + 1 + k, bundles)
+        v = behind(k)
         for j in range(per):
             source = v * per + j
 
@@ -292,13 +296,17 @@
                 low_half, update[2 * half : 3 * half], update[3 * half :]
             )
 
-        @pl.loop(1, slabs)
+        @pl.loop(0, bundles)
         def _(k):
-            to = lax.rem(me + slabs - k, slabs)
-            send2[h, to] = inc_f32[
-                h, pl.ds(pl.multiple_of(to * part_rows, 16), part_rows), :
-            ].astype(jnp.bfloat16)
-            backward(h, to).start()
+            for j in range(per):
+                to = ahead(k) * per + j
+                send2[h, to] = inc_f32[
+                    h, pl.ds(pl.multiple_of(to * part_rows, 16), part_rows), :
+                ].astype(jnp.bfloat16)
+
+                @pl.when(to != me)
+                def _():
+                    backward(h, to).start()
 
     def finish(h, s, low):
         base = s * rows + h * part_rows
@@ -313,19 +321,18 @@
             out[:, at] = bg[:, at] + part
 
     for h in range(parts):
-        finish(
-            h,
-            me,
-            inc_f32[h, pl.ds(pl.multiple_of(me * part_rows, 16), part_rows), :].astype(
-                jnp.bfloat16
-            ),
-        )
-
-        @pl.loop(1, slabs)
+        recv2[h, me] = send2[h, me]
+
+        @pl.loop(0, bundles)
         def _(k):
-            source = lax.rem(me + k, slabs)
-            back(h, source).wait_recv()
-            finish(h, source, recv2[h, source])
+            for j in range(per):
+                source = behind(k) * per + j
+
+                @pl.when(source != me)
+                def _():
+                    back(h, source).wait_recv()
+
+                finish(h, source, recv2[h, source])
 
     @pl.loop(1, slabs)
     def _(k):

time: 31.4 us -> 31.3 us (level)
  no operation moved by 1% of the time
where the time goes in v4:
time: 31.3 us; the launch traced here: 31.1 us
  Pallas kernels  29.7 us (95%)
  local copies, waits for them, and re-layouts  0.8 us (3%)
  between operations  0.66 us (2%)
    pallas_call x1, Pallas kernels, local(): pl.pallas_call(functools.partial(kernel, slabs, groups, parts), out_shape...  29.7 us
    unnamed x1, local copies, waits for them, and re-layouts  0.8 us

profile of v4, /device:TPU:0, one launch (start us, length us, event | category | flops | bytes accessed | tf_op | source)
XLA Modules:
  0.0 31.1 jit_solution(12719500030676055747)
XLA Ops:
  0.7 29.7 %shard_map.82 = f32[4,32768]{1,0:T(4,128)S(1)} custom-call(f32[4,32768]{1,0:T(4,128)} %bg_hbm.1, bf16[64,1024]{1,0:T(8,128)(2,1)} %bitcast.7, f32[1,1024]{1,0:T(1,128)} %readings_hbm.1, f32[1,1024]{1,0:T(1,128)} %noise_hbm.1, s32[1,1024]{1,0:T(1,128)} %location_hbm.1, s32[1,1]{1,0:T(1,128)S(6)} %copy.11.tally, s32[8,32]{1,0:T(8,128)} %bitcast.8, f32[8,32]{1,0:T(8,128)} %bitcast.9), custom_call_target="tpu_custom_call" | custom-call | flops 200000000 | bytes 2000000 | tf_op jit(solution)/shard_map/pallas_call | solution.py:375
  30.3 0.8 %copy.10 = f32[4,32768]{1,0:T(4,128)} copy(f32[4,32768]{1,0:T(4,128)S(1)} %shard_map.82) | data formatting | bytes 1048576

commit v5 on v4

--- a/solution.py
+++ b/solution.py
@@ -368,7 +368,7 @@
         slots = measurement_grid_location.shape[1]
         chunks = slots // LANES
         blocks, links = coupling_listing.shape[1:]
-        parts = 2 if rows % 32 == 0 else 1
+        parts = 4 if rows % 64 == 0 else 1
         smem = pl.BlockSpec(memory_space=pltpu.SMEM)
         hbm = pl.BlockSpec(memory_space=pl.ANY)
         f32, bf16, i32 = jnp.float32, jnp.bfloat16, jnp.int32

time: 31.3 us -> 32 us (1.022)
  Pallas kernels: 29.7 us -> 30.4 us
    pallas_call x1, Pallas kernels: 29.7 us -> 30.4 us  [local(): pl.pallas_call(functools.partial(kernel, slabs, groups, parts), out_shape...]
where the time goes in v5:
time: 32 us; the launch traced here: 31.9 us
  Pallas kernels  30.4 us (95%)
  local copies, waits for them, and re-layouts  0.8 us (2%)
  between operations  0.66 us (2%)
    pallas_call x1, Pallas kernels, local(): pl.pallas_call(functools.partial(kernel, slabs, groups, parts), out_shape...  30.4 us
    unnamed x1, local copies, waits for them, and re-layouts  0.8 us

profile of v5, /device:TPU:0, one launch (start us, length us, event | category | flops | bytes accessed | tf_op | source)
XLA Modules:
  0.0 31.9 jit_solution(13054174251356916055)
XLA Ops:
  0.7 30.4 %shard_map.82 = f32[4,32768]{1,0:T(4,128)S(1)} custom-call(f32[4,32768]{1,0:T(4,128)} %bg_hbm.1, bf16[64,1024]{1,0:T(8,128)(2,1)} %bitcast.7, f32[1,1024]{1,0:T(1,128)} %readings_hbm.1, f32[1,1024]{1,0:T(1,128)} %noise_hbm.1, s32[1,1024]{1,0:T(1,128)} %location_hbm.1, s32[1,1]{1,0:T(1,128)S(6)} %copy.11.tally, s32[8,32]{1,0:T(8,128)} %bitcast.8, f32[8,32]{1,0:T(8,128)} %bitcast.9), custom_call_target="tpu_custom_call" | custom-call | flops 200000000 | bytes 2000000 | tf_op jit(solution)/shard_map/pallas_call | solution.py:375
  31.1 0.8 %copy.10 = f32[4,32768]{1,0:T(4,128)} copy(f32[4,32768]{1,0:T(4,128)S(1)} %shard_map.82) | data formatting | bytes 1048576

commit v6 on v5

--- a/solution.py
+++ b/solution.py
@@ -368,7 +368,7 @@
         slots = measurement_grid_location.shape[1]
         chunks = slots // LANES
         blocks, links = coupling_listing.shape[1:]
-        parts = 4 if rows % 64 == 0 else 1
+        parts = 1
         smem = pl.BlockSpec(memory_space=pltpu.SMEM)
         hbm = pl.BlockSpec(memory_space=pl.ANY)
         f32, bf16, i32 = jnp.float32, jnp.bfloat16, jnp.int32

time: 32 us -> 31.3 us (0.978)
  Pallas kernels: 30.4 us -> 29.7 us
    pallas_call x1, Pallas kernels: 30.4 us -> 29.7 us  [local(): pl.pallas_call(functools.partial(kernel, slabs, groups, parts), out_shape...]
where the time goes in v6:
time: 31.3 us; the launch traced here: 31.2 us
  Pallas kernels  29.7 us (95%)
  local copies, waits for them, and re-layouts  0.8 us (3%)
  between operations  0.66 us (2%)
    pallas_call x1, Pallas kernels, local(): pl.pallas_call(functools.partial(kernel, slabs, groups, parts), out_shape...  29.7 us
    unnamed x1, local copies, waits for them, and re-layouts  0.8 us

profile of v6, /device:TPU:0, one launch (start us, length us, event | category | flops | bytes accessed | tf_op | source)
XLA Modules:
  0.0 31.2 jit_solution(15902680257895371379)
XLA Ops:
  0.7 29.7 %shard_map.82 = f32[4,32768]{1,0:T(4,128)S(1)} custom-call(f32[4,32768]{1,0:T(4,128)} %bg_hbm.1, bf16[64,1024]{1,0:T(8,128)(2,1)} %bitcast.7, f32[1,1024]{1,0:T(1,128)} %readings_hbm.1, f32[1,1024]{1,0:T(1,128)} %noise_hbm.1, s32[1,1024]{1,0:T(1,128)} %location_hbm.1, s32[1,1]{1,0:T(1,128)S(6)} %copy.11.tally, s32[8,32]{1,0:T(8,128)} %bitcast.8, f32[8,32]{1,0:T(8,128)} %bitcast.9), custom_call_target="tpu_custom_call" | custom-call | flops 200000000 | bytes 2000000 | tf_op jit(solution)/shard_map/pallas_call | solution.py:375
  30.4 0.8 %copy.10 = f32[4,32768]{1,0:T(4,128)} copy(f32[4,32768]{1,0:T(4,128)S(1)} %shard_map.82) | data formatting | bytes 1048576
